TPU v7x, 512 devices: a whole 4x8x8 slice. The times are simulated.
512 devices in a mesh: head: 8 (over y), blk: 64 (over z, x, core).
Axes of the slice: x: 4, y: 8, z: 8, core: 2. Of those that a mesh axis runs over, the one named last changes fastest.
Arguments:
- residual: bfloat16 [12288, 2048], P('blk'), may hold values from -100 to 100
- lengths: int32 [64, 6], P('blk'), may hold values from 1 to 96, 192 in all within a row
- token_adapter_index: int32 [12288, 1], P('blk'), may hold values from 0 to 63; in each aligned block of 192 rows (0 to 191, 192 to 383, ...) at most 6 rows name the same one
- attention_norm_gain: float32 [2048], replicated, may hold values from 0.1 to 1.9
- query_key_weight: bfloat16 [2048, 4096], P('blk', 'head'), may hold values from -8 to 8
- value_weight: bfloat16 [2048, 2048], P('blk', 'head'), may hold values from -0.125 to 0.125
- head_second_weight: float32 [8], P('head'), may hold values from 0.2 to 0.8
- output_weight: bfloat16 [2048, 2048], P('blk', 'head'), may hold values from -0.125 to 0.125
- adapter_down_maps: bfloat16 [64, 2048, 16], P('blk', 'head'), may hold values from -0.125 to 0.125
- adapter_up_maps: bfloat16 [64, 16, 2048], P('blk'), may hold values from -1.5 to 1.5
- feedforward_norm_gain: float32 [2048], replicated, may hold values from 0.1 to 1.9
- gate_weight: bfloat16 [2048, 5632], P('blk', 'head'), may hold values from -0.125 to 0.125
- up_weight: bfloat16 [2048, 5632], P('blk', 'head'), may hold values from -0.125 to 0.125
- down_weight: bfloat16 [2048, 5632], P('blk', 'head'), may hold values from -0.078125 to 0.078125
Outputs:
- layer_out: bfloat16 [12288, 2048], P('blk', 'head')
Inputs may be any that keep to these rules, and one draw needn't show every extreme that they name: `lengths`: each row sums to 192, and its largest entry is 96. `token_adapter_index`: among the 192 tokens of one block no adapter is named more than 6 times, a bound that some block reaches.
All inputs are finite; a program needn't handle non-finite values.
Results may differ from a plain program's by a relative error of at most 0.011.
Values may be sent and summed in bfloat16 or wider, within the bound.
No kernel may reach another device: no remote copies, remote signals or barrier semaphores. Data moves between devices by JAX's collectives and lax.ppermute only.
A program may use at most 64 MiB of HBM per device.

v0:
```python
import jax
import jax.numpy as jnp
from jax import lax
from jax.sharding import PartitionSpec as P

HD = 128
adapter_scaling = 2.0
head_shrink = 0.8
neg_large = -1e30


def rms_scale(values, epsilon):
    return values * lax.rsqrt(jnp.mean(values * values, axis=-1, keepdims=True) + epsilon)


def masked_softmax(scores, allowed):
    scores = jnp.where(allowed, scores, neg_large)
    row_peak = jnp.max(scores, axis=-1, keepdims=True)
    raised = jnp.where(allowed, jnp.exp(scores - row_peak), 0.0)
    return raised / jnp.sum(raised, axis=-1, keepdims=True)


def request_mask(lengths_row, length_total):
    ends_at = jnp.cumsum(lengths_row)
    position = jnp.arange(length_total, dtype=jnp.int32)
    request = jnp.sum((position[:, None] >= ends_at[None, :]).astype(jnp.int32), axis=1)
    return (request[:, None] == request[None, :]) & (position[None, :] <= position[:, None])


def diff_head(qk_head, value_head, allowed, lambda_value):
    score_scale = 1.0 / qk_head.shape[-1] ** 0.5
    first_scores = (
        jnp.dot(qk_head[:, 0], qk_head[:, 2].T, precision=lax.Precision.HIGHEST) * score_scale
    )
    second_scores = (
        jnp.dot(qk_head[:, 1], qk_head[:, 3].T, precision=lax.Precision.HIGHEST) * score_scale
    )
    mixed = (
        masked_softmax(first_scores, allowed)
        - lambda_value * masked_softmax(second_scores, allowed)
    ).astype(jnp.bfloat16)
    attended = jnp.dot(mixed, value_head, preferred_element_type=jnp.float32)
    return (rms_scale(attended, 1e-05) * head_shrink).astype(jnp.bfloat16)


def weight_fold(leading, trailing, combine, initial):
    return combine(
        initial,
        (
            lax.all_gather(leading, "blk", axis=0, tiled=True),
            lax.all_gather(trailing, "blk", axis=0, tiled=True),
        ),
        jnp.int32(0),
    )


def head_total(partial_value):
    return lax.psum_scatter(
        partial_value.astype(jnp.bfloat16), "head", scatter_dimension=1, tiled=True
    ).astype(jnp.float32)


def row_products(source):

    def add_rows(totals, pieces, offset):
        return (
            jnp.dot(source, pieces[0], preferred_element_type=jnp.float32),
            jnp.dot(source, pieces[1], preferred_element_type=jnp.float32),
        )

    return add_rows


def per_device(
    residual,
    lengths,
    token_adapter_index,
    attention_norm_gain,
    query_key_weight,
    value_weight,
    head_second_weight,
    output_weight,
    adapter_down_maps,
    adapter_up_maps,
    feedforward_norm_gain,
    gate_weight,
    up_weight,
    down_weight,
):
    tokens = residual.shape[0]
    width = residual.shape[1]
    owners = lax.axis_size("blk")
    capacity = 2 * tokens // owners
    own_width = width // lax.axis_size("head")
    own_begin = lax.axis_index("head") * own_width
    inputs = residual.astype(jnp.float32)
    normed = (rms_scale(inputs, 1e-06) * attention_norm_gain).astype(jnp.bfloat16)
    qk_start = jnp.zeros((tokens, query_key_weight.shape[1]), jnp.float32)
    value_start = jnp.zeros((tokens, value_weight.shape[1]), jnp.float32)
    qk_local, value_local = weight_fold(
        query_key_weight, value_weight, row_products(normed), (qk_start, value_start)
    )
    qk_head = qk_local.reshape(tokens, 4, HD)
    value_head = value_local.astype(jnp.bfloat16)
    allowed = request_mask(lengths[0], tokens)
    head_out = diff_head(qk_head, value_head, allowed, head_second_weight[0])
    chosen = token_adapter_index[:, 0]
    owner_ids = jnp.arange(owners, dtype=jnp.int32)
    member = (chosen[:, None] == owner_ids[None, :]).astype(jnp.int32)
    earlier = jnp.cumsum(member, axis=0) - member
    within = jnp.sum(earlier * member, axis=1)
    target = chosen * capacity + within
    slot_ids = jnp.arange(owners * capacity, dtype=jnp.int32)
    dispatch = (slot_ids[:, None] == target[None, :]).astype(jnp.bfloat16)
    outgoing = jnp.dot(dispatch, head_out, preferred_element_type=jnp.float32).astype(jnp.bfloat16)
    outgoing = outgoing.reshape(owners, capacity, head_out.shape[1])
    received = lax.all_to_all(outgoing, "blk", split_axis=0, concat_axis=0, tiled=True)
    sources = received.shape[0]
    slot_count = received.shape[1]
    flat_heads_output = received.reshape(sources * slot_count, received.shape[2])
    reduced_rank_part = jnp.dot(
        flat_heads_output, adapter_down_maps[0], preferred_element_type=jnp.float32
    )
    reduced_rank_state = lax.psum(reduced_rank_part, "head").astype(jnp.bfloat16)
    adapter_delta = (
        adapter_scaling
        * jnp.dot(reduced_rank_state, adapter_up_maps[0], preferred_element_type=jnp.float32)
    ).astype(jnp.bfloat16)
    returned = lax.all_to_all(
        adapter_delta.reshape(sources, slot_count, width),
        "blk",
        split_axis=0,
        concat_axis=0,
        tiled=True,
    )
    delta_rows = lax.dot_general(
        dispatch,
        returned.reshape(owners * capacity, returned.shape[2]),
        (((0,), (0,)), ((), ())),
        preferred_element_type=jnp.float32,
    )
    delta_own = lax.dynamic_slice_in_dim(delta_rows, own_begin, own_width, 1)
    unit_count = down_weight.shape[1]

    def place_columns(totals, pieces, offset):
        columns = lax.dot_general(
            head_out, pieces[0], (((1,), (1,)), ((), ())), preferred_element_type=jnp.float32
        )
        return (columns, pieces[1])

    projected_start = jnp.zeros((tokens, width), jnp.float32)
    down_start = jnp.zeros((width, unit_count), jnp.bfloat16)
    projected, down_full = weight_fold(
        output_weight, down_weight, place_columns, (projected_start, down_start)
    )
    own_mid = (
        lax.dynamic_slice_in_dim(inputs, own_begin, own_width, 1)
        + head_total(projected)
        + delta_own
    )
    mid_full = lax.all_gather(own_mid.astype(jnp.bfloat16), "head", axis=1, tiled=True)
    ffn_in = (rms_scale(mid_full.astype(jnp.float32), 1e-06) * feedforward_norm_gain).astype(
        jnp.bfloat16
    )
    gate_start = jnp.zeros((tokens, gate_weight.shape[1]), jnp.float32)
    up_start = jnp.zeros((tokens, up_weight.shape[1]), jnp.float32)
    gate_act, upward = weight_fold(
        gate_weight, up_weight, row_products(ffn_in), (gate_start, up_start)
    )
    hidden_units = (jax.nn.silu(gate_act) * upward).astype(jnp.bfloat16)
    ffn_part = lax.dot_general(
        hidden_units, down_full, (((1,), (1,)), ((), ())), preferred_element_type=jnp.float32
    )
    return (own_mid + head_total(ffn_part)).astype(jnp.bfloat16)


def solution(mesh):
    return jax.shard_map(
        per_device,
        mesh=mesh,
        in_specs=(
            P("blk", None),
            P("blk", None),
            P("blk", None),
            P(),
            P("blk", "head"),
            P("blk", "head"),
            P("head"),
            P("blk", "head"),
            P("blk", "head", None),
            P("blk", None, None),
            P(),
            P("blk", "head"),
            P("blk", "head"),
            P("blk", "head"),
        ),
        out_specs=P("blk", "head"),
        check_vma=False,
    )
```

profile of v0, /device:TPU:2, one launch (start us, length us, event | category | flops | bytes accessed | tf_op | source)
XLA Modules:
  0.0 619.7 jit_solution(7784527970061427897)
XLA Ops:
  6.5 0.0 copy-start
  6.5 0.0 all-gather.7.cloned.1.call-start
  6.5 0.7 all-gather.7.cloned.1.call-update
  7.3 0.0 all-gather.9.cloned.1.call-start
  7.3 0.7 all-gather.9.cloned.1.call-update
  8.0 0.0 all-gather.11.cloned.1.call-start
  8.1 0.7 all-gather.11.cloned.1.call-update
  8.7 0.0 reduce-scatter.3.cloned.1.call-start
  8.8 0.8 reduce-window.18
  9.6 0.1 convert_reduce_fusion
  10.4 1.4 multiply_reduce_fusion
  11.7 86.2 %all-gather.7.cloned.1.call-done = bf16[2048,512]{1,0:T(8,128)(2,1)} async-done(((bf16[32,512]{1,0:T(8,128)(2,1)}), bf16[2048,512]{1,0:T(8,128)(2,1)}) %all-gather.7.cloned.1.call-update) | async-done | bytes 2097168 | tf_op jit(solution)/shard_map/all_gather | solution.py:50
  97.9 2.5 fusion.14
  100.4 0.0 copy-start.1
  100.4 0.0 copy-start.5
  100.4 0.1 reshape.92
  100.6 0.3 fusion.40
  100.8 0.4 fusion.42
  101.2 0.4 fusion.41
  101.6 0.1 fusion.22
  101.7 79.3 %all-gather.9.cloned.1.call-done = bf16[2048,256]{1,0:T(8,128)(2,1)} async-done(((bf16[32,256]{1,0:T(8,128)(2,1)}), bf16[2048,256]{1,0:T(8,128)(2,1)}) %all-gather.9.cloned.1.call-update) | async-done | bytes 1048592 | tf_op jit(solution)/shard_map/all_gather | solution.py:51
  181.0 0.0 copy-done.5
  181.0 2.0 multiply_reduce_fusion.1
  182.9 0.0 copy-start.3
  183.0 81.1 %all-gather.11.cloned.1.call-done = bf16[2048,256]{1,0:T(8,128)(2,1)} async-done(((bf16[32,256]{1,0:T(8,128)(2,1)}), bf16[2048,256]{1,0:T(8,128)(2,1)}) %all-gather.11.cloned.1.call-update) | async-done | bytes 1048592 | tf_op jit(solution)/shard_map/all_gather | solution.py:50
  264.1 2.7 convolution_convert_fusion.1
  266.8 0.0 reduce-scatter.3.cloned.1.call-update
  266.8 0.0 all-gather.13.cloned.1.call-start
  266.9 0.5 all-gather.13.cloned.1.call-update
  267.4 0.0 all-gather.15.cloned.1.call-start
  267.4 0.5 all-gather.15.cloned.1.call-update
  268.0 0.0 all-gather.17.cloned.1.call-start
  268.0 0.7 all-gather.17.cloned.1.call-update
  268.8 0.6 reduce-window.19
  269.4 0.2 slice_reduce_fusion
  269.6 0.1 bitcast_bitcast_fusion
  269.8 0.3 convolution_convert_fusion.2
  270.0 0.1 reshape.95
  270.1 19.7 %all_to_all.10 = bf16[64,6,256]{2,1,0:T(8,128)(2,1)S(1)} all-to-all(bf16[64,6,256]{2,1,0:T(8,128)(2,1)S(1)} %reshape.95), channel_id=1, replica_groups=mesh['head'=8,'blk'=64] {'blk'}, dimensions={0} | all-to-all | bytes 393216 | tf_op jit(solution)/shard_map/all_to_all | solution.py:117
  289.8 0.1 reshape.96
  289.9 0.2 fusion.35
  290.1 29.8 %psum.7 = bf16[384,16]{0,1:T(8,128)(2,1)S(1)} all-reduce(f32[384,16]{0,1:T(8,128)S(1)} %fusion.35), channel_id=1, replica_groups=mesh['head'=8,'blk'=64] {'head'}, use_global_device_ids=true, to_apply=%region_12.13 | all-reduce | flops 6144 | bytes 36864 | tf_op jit(solution)/shard_map/psum | solution.py:124
  319.8 0.0 copy-done
  319.9 0.6 multiply_convert_fusion
  320.4 1.6 reshape.97
  322.0 5.6 all-to-all-start.1
  327.7 0.0 reduce-scatter.5.cloned.1.call-start
  327.7 1.4 convert_element_type.59
  329.1 54.3 %all-to-all-done.1 = bf16[64,6,2048]{2,1,0:T(8,128)(2,1)S(1)} async-done(((bf16[64,6,2048]{2,1,0:T(8,128)(2,1)}), bf16[64,6,2048]{2,1,0:T(8,128)(2,1)S(1)}, u32[]{:S(2)}, u32[]{:S(2)}) %all-to-all-start.1) | async-done | bytes 1572896 | tf_op jit(solution)/shard_map/all_to_all | solution.py:129
  383.4 1.4 reshape.98
  384.8 2.0 fusion.12
  386.9 0.0 copy-start.6
  386.9 0.0 reduce-scatter.3.cloned.1.call-done
  386.9 1.0 fusion.37
  388.0 26.0 %all_gather.24 = bf16[192,2048]{1,0:T(8,128)(2,1)S(1)} all-gather(bf16[192,256]{1,0:T(8,128)(2,1)S(1)} %fusion.37), channel_id=1, replica_groups=mesh['head'=8,'blk'=64] {'head'}, dimensions={1}, use_global_device_ids=true | all-gather | bytes 884736 | tf_op jit(solution)/shard_map/all_gather | solution.py:161
  413.9 0.2 fusion
  414.2 0.0 all-gather.13.cloned.1.call-done
  414.2 2.7 fusion.17
  417.0 64.8 %all-gather.15.cloned.1.call-done = bf16[2048,704]{1,0:T(8,128)(2,1)} async-done(((bf16[32,704]{1,0:T(8,128)(2,1)}), bf16[2048,704]{1,0:T(8,128)(2,1)}) %all-gather.15.cloned.1.call-update) | async-done | bytes 2883600 | tf_op jit(solution)/shard_map/all_gather | solution.py:51
  481.7 85.3 %all-gather.17.cloned.1.call-done = bf16[2048,704]{1,0:T(8,128)(2,1)} async-done(((bf16[32,704]{1,0:T(8,128)(2,1)}), bf16[2048,704]{1,0:T(8,128)(2,1)}) %all-gather.17.cloned.1.call-update) | async-done | bytes 2883600 | tf_op jit(solution)/shard_map/all_gather | solution.py:51
  567.0 5.7 convolution_convert_fusion
  572.7 0.0 reduce-scatter.5.cloned.1.call-update
  572.8 38.4 %reduce-scatter.5.cloned.1.call-done = bf16[192,256]{1,0:T(8,128)(2,1)} async-done(((bf16[192,2048]{1,0:T(8,128)(2,1)}), bf16[192,256]{1,0:T(8,128)(2,1)}) %reduce-scatter.5.cloned.1.call-update) | async-done | bytes 98320 | tf_op jit(solution)/shard_map/reduce_scatter | solution.py:58
  611.2 1.7 add_convert_fusion
  (16 shorter events, 0.1 us)
Async XLA Ops:
  6.5 313.3 %copy-start = (bf16[1,16,2048]{2,1,0:T(8,128)(2,1)S(1)}, bf16[1,16,2048]{2,1,0:T(8,128)(2,1)}, u32[]{:S(2)}) copy-start(bf16[1,16,2048]{2,1,0:T(8,128)(2,1)} %param.23) | copy-start | bytes 196612
  6.5 91.4 %all-gather.7.cloned.1.call-start = ((), (), s32[]{:S(2)}) async-start(), calls=%async_computation.4 | async-start | bytes 2129920 | tf_op jit(solution)/shard_map/all_gather | solution.py:50
  7.3 173.7 %all-gather.9.cloned.1.call-start = ((), (), s32[]{:S(2)}) async-start(), calls=%async_computation.5 | async-start | bytes 1064960 | tf_op jit(solution)/shard_map/all_gather | solution.py:51
  8.0 256.1 %all-gather.11.cloned.1.call-start = ((), (), s32[]{:S(2)}) async-start(), calls=%async_computation.6 | async-start | bytes 1064960 | tf_op jit(solution)/shard_map/all_gather | solution.py:50
  8.7 378.2 %reduce-scatter.3.cloned.1.call-start = ((), (), s32[]{:S(2)}) async-start(), calls=%async_computation.7 | async-start | bytes 884736 | tf_op jit(solution)/shard_map/reduce_scatter | solution.py:58
  100.4 80.6 %copy-start.1 = (bf16[192,2048]{1,0:T(8,128)(2,1)S(1)}, bf16[192,2048]{1,0:T(8,128)(2,1)}, u32[]{:S(2)}) copy-start(bf16[192,2048]{1,0:T(8,128)(2,1)} %param.14) | copy-start | bytes 2359300
  100.4 80.6 %copy-start.5 = (f32[2048]{0:T(1024)S(1)}, f32[2048]{0:T(1024)}, u32[]{:S(2)}) copy-start(f32[2048]{0:T(1024)} %param.17) | copy-start | bytes 24580
  182.9 85.8 %copy-start.3 = (s32[192,1]{0,1:T(1,128)S(1)}, s32[192,1]{0,1:T(1,128)}, u32[]{:S(2)}) copy-start(s32[192,1]{0,1:T(1,128)} %param.16) | copy-start | bytes 2308
  266.8 23.1 %copy-start.4 = (bf16[1,256,16]{1,2,0:T(8,128)(2,1)S(1)}, bf16[1,256,16]{1,2,0:T(8,128)(2,1)}, u32[]{:S(2)}) copy-start(bf16[1,256,16]{1,2,0:T(8,128)(2,1)} %param.22) | copy-start | bytes 24580
  266.8 147.4 %all-gather.13.cloned.1.call-start = ((), (), s32[]{:S(2)}) async-start(), calls=%async_computation.8 | async-start | bytes 3194880 | tf_op jit(solution)/shard_map/all_gather | solution.py:50
  267.4 214.3 %all-gather.15.cloned.1.call-start = ((), (), s32[]{:S(2)}) async-start(), calls=%async_computation.9 | async-start | bytes 3194880 | tf_op jit(solution)/shard_map/all_gather | solution.py:51
  268.0 299.0 %all-gather.17.cloned.1.call-start = ((), (), s32[]{:S(2)}) async-start(), calls=%async_computation.10 | async-start | bytes 3194880 | tf_op jit(solution)/shard_map/all_gather | solution.py:51
  322.0 61.4 %all-to-all-start.1 = ((bf16[64,6,2048]{2,1,0:T(8,128)(2,1)}), bf16[64,6,2048]{2,1,0:T(8,128)(2,1)S(1)}, u32[]{:S(2)}, u32[]{:S(2)}) async-start(bf16[64,6,2048]{2,1,0:T(8,128)(2,1)} %reshape.97), calls=%async_computation.2 | async-start | bytes 4194304 | tf_op jit(solution)/shard_map/all_to_all | solution.py:129
  327.7 283.5 %reduce-scatter.5.cloned.1.call-start = ((), (), s32[]{:S(2)}) async-start(), calls=%async_computation.11 | async-start | bytes 884736 | tf_op jit(solution)/shard_map/reduce_scatter | solution.py:58
  386.9 27.3 %copy-start.6 = (f32[2048]{0:T(1024)S(1)}, f32[2048]{0:T(1024)}, u32[]{:S(2)}) copy-start(f32[2048]{0:T(1024)} %param.24) | copy-start | bytes 24580
  416.9 194.2 %copy-start.2 = (bf16[192,256]{1,0:T(8,128)(2,1)S(1)}, bf16[192,256]{1,0:T(8,128)(2,1)}, u32[]{:S(2)}) copy-start(bf16[192,256]{1,0:T(8,128)(2,1)} %reduce-scatter.3.cloned.1.call-done) | copy-start | bytes 294916
Sparse Core Ops, SparseCore 0:
  10.7 87.1 all-gather.6
  101.3 79.6 all-gather.8
  184.3 79.7 all-gather.10
  266.9 38.3 reduce-scatter.2
  309.0 88.1 all-gather.12
  400.9 80.8 all-gather.14
  485.6 81.3 all-gather.16
  572.9 38.2 reduce-scatter.4
where the time goes:
time: 620 us
  waiting for transfers between devices  493 us (80%)
  blocking collectives  75.5 us (12%)
  matrix products  19.4 us (3%)
  between operations  14.3 us (2%)
  other arithmetic  7.53 us (1%)
    all_gather x3, waiting for transfers between devices, weight_fold(): lax.all_gather(trailing, 'blk', axis=0, tiled=True)  229 us
    all_gather x3, waiting for transfers between devices, weight_fold(): lax.all_gather(leading, 'blk', axis=0, tiled=True)  167 us
    all_to_all x1, waiting for transfers between devices, per_device(): lax.all_to_all(adapter_delta.reshape(sources, slot_count, width), 'blk',...  54.3 us
    reduce_scatter x2, waiting for transfers between devices, head_total(): lax.psum_scatter(partial_value.astype(jnp.bfloat16), 'head', scatter_dime...  38.4 us
    psum x1, blocking collectives, per_device(): lax.psum(reduced_rank_part, 'head').astype(jnp.bfloat16)  29.8 us
    all_gather x1, blocking collectives, per_device(): lax.all_gather(own_mid.astype(jnp.bfloat16), 'head', axis=1, tiled=True)  26 us
    all_to_all x1, blocking collectives, per_device(): lax.all_to_all(outgoing, 'blk', split_axis=0, concat_axis=0, tiled=True)  19.7 us
  transfers between devices with their start and end apart: 9, of which 7 were waited for; matrix products, arithmetic and copies ran while one was open for 3% of the time, Pallas kernels for 0%

commit v1 on v0

--- a/solution.py
+++ b/solution.py
@@ -121,7 +121,7 @@
     reduced_rank_part = jnp.dot(
         flat_heads_output, adapter_down_maps[0], preferred_element_type=jnp.float32
     )
-    reduced_rank_state = lax.psum(reduced_rank_part, "head").astype(jnp.bfloat16)
+    reduced_rank_state = lax.all_gather(reduced_rank_part, "head").sum(axis=0).astype(jnp.bfloat16)
     adapter_delta = (
         adapter_scaling
         * jnp.dot(reduced_rank_state, adapter_up_maps[0], preferred_element_type=jnp.float32)

time: 620 us -> 620 us (level)
  blocking collectives: 75.5 us -> 52.1 us
  waiting for transfers between devices: 493 us -> 508 us
  starting transfers between devices: 5.91 us -> 13.5 us
    psum x1 -> x0, blocking collectives: 29.8 us -> none  [per_device(): lax.psum(reduced_rank_part, 'head').astype(jnp.bfloat16)]
    all_gather x0 -> x1, blocking collectives: none -> 26 us  [per_device(): lax.all_gather(reduced_rank_part, 'head').sum(axis=0).astype(jnp.bfloat16)]
    all_to_all x1 -> x0, blocking collectives: 19.7 us -> none  [per_device(): lax.all_to_all(outgoing, 'blk', split_axis=0, concat_axis=0, tiled=True)]
    all_to_all x0 -> x1, waiting for transfers between devices: none -> 11.5 us  [per_device(): lax.all_to_all(outgoing, 'blk', split_axis=0, concat_axis=0, tiled=True)]
    all_to_all x0 -> x1, starting transfers between devices: none -> 7.68 us  [per_device(): lax.all_to_all(outgoing, 'blk', split_axis=0, concat_axis=0, tiled=True)]
  transfers between devices with their start and end apart: 9 -> 10, of which waited for: 7 -> 8; matrix products, arithmetic and copies ran while one was open for 3% -> 3% of each run, Pallas kernels for 0% -> 0%
where the time goes in v1:
time: 620 us; the launch traced here: 619 us
  waiting for transfers between devices  508 us (82%)
  blocking collectives  52.1 us (8%)
  matrix products  19.4 us (3%)
  between operations  14.4 us (2%)
  starting transfers between devices  13.5 us (2%)
  other arithmetic  7.59 us (1%)
    all_gather x3, waiting for transfers between devices, weight_fold(): lax.all_gather(trailing, 'blk', axis=0, tiled=True)  234 us
    all_gather x3, waiting for transfers between devices, weight_fold(): lax.all_gather(leading, 'blk', axis=0, tiled=True)  167 us
    all_to_all x1, waiting for transfers between devices, per_device(): lax.all_to_all(adapter_delta.reshape(sources, slot_count, width), 'blk',...  53 us
    reduce_scatter x2, waiting for transfers between devices, head_total(): lax.psum_scatter(partial_value.astype(jnp.bfloat16), 'head', scatter_dime...  38.4 us
    all_gather x1, blocking collectives, per_device(): lax.all_gather(own_mid.astype(jnp.bfloat16), 'head', axis=1, tiled=True)  26.1 us
    all_gather x1, blocking collectives, per_device(): lax.all_gather(reduced_rank_part, 'head').sum(axis=0).astype(jnp.bfloat16)  26 us
  transfers between devices with their start and end apart: 10, of which 8 were waited for; matrix products, arithmetic and copies ran while one was open for 3% of the time, Pallas kernels for 0%

profile of v1, /device:TPU:2, one launch (start us, length us, event | category | flops | bytes accessed | tf_op | source)
XLA Modules:
  0.0 619.5 jit_solution(2653456534404462558)
XLA Ops:
  6.5 0.0 all-gather.8.cloned.1.call-start
  6.5 0.7 all-gather.8.cloned.1.call-update
  7.3 0.0 all-gather.10.cloned.1.call-start
  7.3 0.7 all-gather.10.cloned.1.call-update
  8.0 0.0 all-gather.12.cloned.1.call-start
  8.1 0.7 all-gather.12.cloned.1.call-update
  8.7 0.0 reduce-scatter.3.cloned.1.call-start
  8.8 0.8 reduce-window.18
  9.6 0.1 convert_reduce_fusion
  10.4 1.4 multiply_reduce_fusion
  11.7 86.2 %all-gather.8.cloned.1.call-done = bf16[2048,512]{1,0:T(8,128)(2,1)} async-done(((bf16[32,512]{1,0:T(8,128)(2,1)}), bf16[2048,512]{1,0:T(8,128)(2,1)}) %all-gather.8.cloned.1.call-update) | async-done | bytes 2097168 | tf_op jit(solution)/shard_map/all_gather | solution.py:50
  97.9 2.5 fusion.14
  100.4 0.0 copy-start.1
  100.4 0.0 copy-start.5
  100.4 0.1 reshape.92
  100.6 0.3 fusion.40
  100.8 0.4 fusion.42
  101.2 0.4 fusion.41
  101.6 0.1 fusion.22
  101.7 79.3 %all-gather.10.cloned.1.call-done = bf16[2048,256]{1,0:T(8,128)(2,1)} async-done(((bf16[32,256]{1,0:T(8,128)(2,1)}), bf16[2048,256]{1,0:T(8,128)(2,1)}) %all-gather.10.cloned.1.call-update) | async-done | bytes 1048592 | tf_op jit(solution)/shard_map/all_gather | solution.py:51
  181.0 0.0 copy-done.5
  181.0 2.0 multiply_reduce_fusion.1
  182.9 0.0 copy-start.3
  183.0 81.1 %all-gather.12.cloned.1.call-done = bf16[2048,256]{1,0:T(8,128)(2,1)} async-done(((bf16[32,256]{1,0:T(8,128)(2,1)}), bf16[2048,256]{1,0:T(8,128)(2,1)}) %all-gather.12.cloned.1.call-update) | async-done | bytes 1048592 | tf_op jit(solution)/shard_map/all_gather | solution.py:50
  264.1 2.7 convolution_convert_fusion.1
  266.8 0.0 reduce-scatter.3.cloned.1.call-update
  266.8 0.0 all-gather.14.cloned.1.call-start
  266.9 0.5 all-gather.14.cloned.1.call-update
  267.4 0.0 all-gather.16.cloned.1.call-start
  267.4 0.5 all-gather.16.cloned.1.call-update
  268.0 0.6 reduce-window.19
  268.6 0.2 slice_reduce_fusion
  268.9 0.1 bitcast_bitcast_fusion
  269.0 0.3 convolution_convert_fusion.2
  269.3 0.8 reshape.95
  270.1 7.7 %all-to-all-start = ((bf16[64,6,256]{2,1,0:T(8,128)(2,1)}), bf16[64,6,256]{2,1,0:T(8,128)(2,1)S(1)}, u32[]{:S(2)}, u32[]{:S(2)}) async-start(bf16[64,6,256]{2,1,0:T(8,128)(2,1)} %reshape.95), calls=%async_computation.1 | async-start | bytes 524288 | tf_op jit(solution)/shard_map/all_to_all | solution.py:117
  277.8 0.0 all-gather.18.cloned.1.call-start
  277.8 0.7 all-gather.18.cloned.1.call-update
  278.5 11.5 %all-to-all-done = bf16[64,6,256]{2,1,0:T(8,128)(2,1)S(1)} async-done(((bf16[64,6,256]{2,1,0:T(8,128)(2,1)}), bf16[64,6,256]{2,1,0:T(8,128)(2,1)S(1)}, u32[]{:S(2)}, u32[]{:S(2)}) %all-to-all-start) | async-done | bytes 196640 | tf_op jit(solution)/shard_map/all_to_all | solution.py:117
  290.0 0.1 reshape.96
  290.1 0.2 fusion.35
  290.2 26.0 %all-gather = f32[3072,16]{0,1:T(8,128)S(1)} all-gather(f32[384,16]{0,1:T(8,128)S(1)} %fusion.35), channel_id=2, replica_groups=mesh['head'=8,'blk'=64] {'head'}, dimensions={0}, use_global_device_ids=true | all-gather | bytes 221184 | tf_op jit(solution)/shard_map/all_gather | solution.py:124
  316.2 0.1 bitcast_reduce_fusion
  316.3 0.6 multiply_convert_fusion
  316.9 1.6 reshape.97
  318.5 5.6 all-to-all-start.1
  324.1 0.0 reduce-scatter.5.cloned.1.call-start
  324.1 1.4 convert_element_type.59
  325.5 53.0 %all-to-all-done.1 = bf16[64,6,2048]{2,1,0:T(8,128)(2,1)S(1)} async-done(((bf16[64,6,2048]{2,1,0:T(8,128)(2,1)}), bf16[64,6,2048]{2,1,0:T(8,128)(2,1)S(1)}, u32[]{:S(2)}, u32[]{:S(2)}) %all-to-all-start.1) | async-done | bytes 1572896 | tf_op jit(solution)/shard_map/all_to_all | solution.py:129
  378.5 1.4 reshape.98
  379.9 2.1 fusion.12
  382.0 0.0 copy-start.6
  382.0 0.0 reduce-scatter.3.cloned.1.call-done
  382.0 1.0 fusion.37
  383.1 26.1 %all_gather.32 = bf16[192,2048]{1,0:T(8,128)(2,1)S(1)} all-gather(bf16[192,256]{1,0:T(8,128)(2,1)S(1)} %fusion.37), channel_id=1, replica_groups=mesh['head'=8,'blk'=64] {'head'}, dimensions={1}, use_global_device_ids=true | all-gather | bytes 884736 | tf_op jit(solution)/shard_map/all_gather | solution.py:161
  409.2 0.2 fusion
  409.4 0.0 all-gather.14.cloned.1.call-done
  409.4 2.7 fusion.17
  412.2 69.4 %all-gather.16.cloned.1.call-done = bf16[2048,704]{1,0:T(8,128)(2,1)} async-done(((bf16[32,704]{1,0:T(8,128)(2,1)}), bf16[2048,704]{1,0:T(8,128)(2,1)}) %all-gather.16.cloned.1.call-update) | async-done | bytes 2883600 | tf_op jit(solution)/shard_map/all_gather | solution.py:51
  481.6 85.3 %all-gather.18.cloned.1.call-done = bf16[2048,704]{1,0:T(8,128)(2,1)} async-done(((bf16[32,704]{1,0:T(8,128)(2,1)}), bf16[2048,704]{1,0:T(8,128)(2,1)}) %all-gather.18.cloned.1.call-update) | async-done | bytes 2883600 | tf_op jit(solution)/shard_map/all_gather | solution.py:51
  566.8 5.7 convolution_convert_fusion
  572.6 0.0 reduce-scatter.5.cloned.1.call-update
  572.6 38.4 %reduce-scatter.5.cloned.1.call-done = bf16[192,256]{1,0:T(8,128)(2,1)} async-done(((bf16[192,2048]{1,0:T(8,128)(2,1)}), bf16[192,256]{1,0:T(8,128)(2,1)}) %reduce-scatter.5.cloned.1.call-update) | async-done | bytes 98320 | tf_op jit(solution)/shard_map/reduce_scatter | solution.py:58
  611.0 1.7 add_convert_fusion
  (19 shorter events, 0.2 us)
Async XLA Ops:
  6.5 309.8 %copy-start = (bf16[1,16,2048]{2,1,0:T(8,128)(2,1)S(1)}, bf16[1,16,2048]{2,1,0:T(8,128)(2,1)}, u32[]{:S(2)}) copy-start(bf16[1,16,2048]{2,1,0:T(8,128)(2,1)} %param.23) | copy-start | bytes 196612
  6.5 91.4 %all-gather.8.cloned.1.call-start = ((), (), s32[]{:S(2)}) async-start(), calls=%async_computation.4 | async-start | bytes 2129920 | tf_op jit(solution)/shard_map/all_gather | solution.py:50
  7.3 173.7 %all-gather.10.cloned.1.call-start = ((), (), s32[]{:S(2)}) async-start(), calls=%async_computation.5 | async-start | bytes 1064960 | tf_op jit(solution)/shard_map/all_gather | solution.py:51
  8.0 256.1 %all-gather.12.cloned.1.call-start = ((), (), s32[]{:S(2)}) async-start(), calls=%async_computation.6 | async-start | bytes 1064960 | tf_op jit(solution)/shard_map/all_gather | solution.py:50
  8.7 373.3 %reduce-scatter.3.cloned.1.call-start = ((), (), s32[]{:S(2)}) async-start(), calls=%async_computation.7 | async-start | bytes 884736 | tf_op jit(solution)/shard_map/reduce_scatter | solution.py:58
  100.4 80.6 %copy-start.1 = (bf16[192,2048]{1,0:T(8,128)(2,1)S(1)}, bf16[192,2048]{1,0:T(8,128)(2,1)}, u32[]{:S(2)}) copy-start(bf16[192,2048]{1,0:T(8,128)(2,1)} %param.14) | copy-start | bytes 2359300
  100.4 80.6 %copy-start.5 = (f32[2048]{0:T(1024)S(1)}, f32[2048]{0:T(1024)}, u32[]{:S(2)}) copy-start(f32[2048]{0:T(1024)} %param.17) | copy-start | bytes 24580
  182.9 85.0 %copy-start.3 = (s32[192,1]{0,1:T(1,128)S(1)}, s32[192,1]{0,1:T(1,128)}, u32[]{:S(2)}) copy-start(s32[192,1]{0,1:T(1,128)} %param.16) | copy-start | bytes 2308
  266.8 23.3 %copy-start.4 = (bf16[1,256,16]{1,2,0:T(8,128)(2,1)S(1)}, bf16[1,256,16]{1,2,0:T(8,128)(2,1)}, u32[]{:S(2)}) copy-start(bf16[1,256,16]{1,2,0:T(8,128)(2,1)} %param.22) | copy-start | bytes 24580
  266.8 142.6 %all-gather.14.cloned.1.call-start = ((), (), s32[]{:S(2)}) async-start(), calls=%async_computation.8 | async-start | bytes 3194880 | tf_op jit(solution)/shard_map/all_gather | solution.py:50
  267.4 214.2 %all-gather.16.cloned.1.call-start = ((), (), s32[]{:S(2)}) async-start(), calls=%async_computation.9 | async-start | bytes 3194880 | tf_op jit(solution)/shard_map/all_gather | solution.py:51
  270.1 19.9 %all-to-all-start = ((bf16[64,6,256]{2,1,0:T(8,128)(2,1)}), bf16[64,6,256]{2,1,0:T(8,128)(2,1)S(1)}, u32[]{:S(2)}, u32[]{:S(2)}) async-start(bf16[64,6,256]{2,1,0:T(8,128)(2,1)} %reshape.95), calls=%async_computation.1 | async-start | bytes 524288 | tf_op jit(solution)/shard_map/all_to_all | solution.py:117
  277.8 289.1 %all-gather.18.cloned.1.call-start = ((), (), s32[]{:S(2)}) async-start(), calls=%async_computation.10 | async-start | bytes 3194880 | tf_op jit(solution)/shard_map/all_gather | solution.py:51
  318.5 60.0 %all-to-all-start.1 = ((bf16[64,6,2048]{2,1,0:T(8,128)(2,1)}), bf16[64,6,2048]{2,1,0:T(8,128)(2,1)S(1)}, u32[]{:S(2)}, u32[]{:S(2)}) async-start(bf16[64,6,2048]{2,1,0:T(8,128)(2,1)} %reshape.97), calls=%async_computation.2 | async-start | bytes 4194304 | tf_op jit(solution)/shard_map/all_to_all | solution.py:129
  324.1 286.9 %reduce-scatter.5.cloned.1.call-start = ((), (), s32[]{:S(2)}) async-start(), calls=%async_computation.11 | async-start | bytes 884736 | tf_op jit(solution)/shard_map/reduce_scatter | solution.py:58
  382.0 27.4 %copy-start.6 = (f32[2048]{0:T(1024)S(1)}, f32[2048]{0:T(1024)}, u32[]{:S(2)}) copy-start(f32[2048]{0:T(1024)} %param.24) | copy-start | bytes 24580
  412.2 198.8 %copy-start.2 = (bf16[192,256]{1,0:T(8,128)(2,1)S(1)}, bf16[192,256]{1,0:T(8,128)(2,1)}, u32[]{:S(2)}) copy-start(bf16[192,256]{1,0:T(8,128)(2,1)} %reduce-scatter.3.cloned.1.call-done) | copy-start | bytes 294916
Sparse Core Ops, SparseCore 0:
  10.7 87.1 all-gather.7
  101.3 79.6 all-gather.9
  184.3 79.7 all-gather.11
  266.9 38.4 reduce-scatter.2
  309.1 87.0 all-gather.13
  399.9 81.5 all-gather.15
  485.4 81.3 all-gather.17
  572.7 38.2 reduce-scatter.4
